TPU v7x, 32 devices: a whole 2x2x4 slice. The times are simulated.
32 devices in a mesh: seq: 8 (over z, y), head: 4 (over x, core).
Axes of the slice: x: 2, y: 2, z: 4, core: 2. Of those that a mesh axis runs over, the one named last changes fastest.
Arguments:
- queries: bfloat16 [2048, 3072], P('seq', 'head'), may hold values from -8 to 8
- key_states: bfloat16 [2048, 3072], P('seq', 'head'), may hold values from -8 to 8
- value_states: bfloat16 [2048, 3072], P('seq', 'head'), may hold values from -12 to 12
- level_offsets: int32 [3, 24], P(None, 'head'), may hold values from 0 to 31
- out_weight: bfloat16 [3072, 5120], P(None, 'head'), may hold values from -0.109375 to 0.109375
Outputs:
- layer_output: bfloat16 [2048, 5120], P('seq', 'head')
All inputs are finite; a program needn't handle non-finite values.
Results may differ from a plain program's by a relative error of at most 0.0057.
Values may be sent and summed in bfloat16 or wider, within the bound.
A program may use at most 64 MiB of HBM per device.

v0:
```python
import jax
import jax.numpy as jnp
from jax import lax
from jax.sharding import PartitionSpec as P

RATE_MID = 8
RATE_TOP = 32
SEG_ROWS = 1024


NEG_FILL = -1e30


def from_behind(array, axis, by):
    peers = lax.axis_size(axis)
    pairs = [(i, i + by) for i in range(peers) if 0 <= i + by < peers]
    return lax.ppermute(array, axis, pairs)


def pick_rows(states, chooser, spacing):
    row_count, head_count, head_width = states.shape
    grouped = states.reshape(row_count // spacing, spacing, head_count, head_width)
    return jnp.einsum("nrhd,rh->nhd", grouped, chooser, preferred_element_type=jnp.float32).astype(
        jnp.bfloat16
    )


def attend(query_rows, key_rows, value_rows, allowed, scale_factor):
    scores = (
        jnp.einsum("qhd,khd->hqk", query_rows, key_rows, preferred_element_type=jnp.float32)
        * scale_factor
    )
    scores = jnp.where(allowed[None], scores, NEG_FILL)
    highest = jnp.max(scores, axis=2, keepdims=True)
    weights = jnp.exp(scores - highest)
    totals = jnp.sum(weights, axis=2, keepdims=True)
    shares = (weights / totals).astype(jnp.bfloat16)
    result = jnp.einsum("hqk,khd->qhd", shares, value_rows, preferred_element_type=jnp.float32)
    return (result, (highest + jnp.log(totals))[:, :, 0].T)


def lower_segment(pair_rows, span_devices):
    holding = pair_rows
    for bit_no in range(span_devices.bit_length() - 1):
        arrived = from_behind(holding, "seq", 2**bit_no)
        holding = jnp.concatenate([arrived, holding], axis=0)
    return holding


def lower_segment_top(pair_rows, span_devices):
    holding = pair_rows
    for bit_no in range(span_devices.bit_length() - 1):
        arrived = from_behind(holding, "seq", 2**bit_no)
        holding = jnp.concatenate([arrived, holding], axis=0)
    return holding


def segment_mask(sparse_count, span_devices, position):
    shape_pair = (sparse_count, span_devices * sparse_count)
    query_index = lax.broadcasted_iota(jnp.int32, shape_pair, 0)
    key_index = lax.broadcasted_iota(jnp.int32, shape_pair, 1)
    lowest = (span_devices - 1 - position) * sparse_count
    return (key_index >= lowest) & (key_index <= (span_devices - 1) * sparse_count + query_index)


def spread_back(level_out, level_lse, chooser):
    picked = chooser.astype(jnp.float32)
    sparse_count, head_count, head_width = level_out.shape
    row_count = sparse_count * chooser.shape[0]
    full_out = (level_out[:, None, :, :] * picked[None, :, :, None]).reshape(
        row_count, head_count, head_width
    )
    full_lse = jnp.where(chooser[None], level_lse[:, None, :], NEG_FILL).reshape(
        row_count, head_count
    )
    return (full_out, full_lse)


def level_setup(query_all, key_all, value_all, offset_row, spacing):
    head_count = query_all.shape[1]
    chooser = (
        lax.broadcasted_iota(jnp.int32, (spacing, head_count), 0) == (offset_row % spacing)[None, :]
    )
    chooser_bf = chooser.astype(jnp.bfloat16)
    query_rows = pick_rows(query_all, chooser_bf, spacing)
    pair_rows = jnp.stack(
        [pick_rows(key_all, chooser_bf, spacing), pick_rows(value_all, chooser_bf, spacing)], axis=1
    )
    return (chooser, query_rows, pair_rows)


def local(queries, key_states, value_states, level_offsets, out_weight):
    row_count = queries.shape[0]
    head_count = level_offsets.shape[1]
    head_width = queries.shape[1] // head_count
    scale_factor = head_width ** (-0.5)
    seq_count = lax.axis_size("seq")
    seq_index = lax.axis_index("seq")
    query_all = queries.reshape(row_count, head_count, head_width)
    key_all = key_states.reshape(row_count, head_count, head_width)
    value_all = value_states.reshape(row_count, head_count, head_width)
    full_outs = []
    full_lses = []
    for level_no, spacing in enumerate((1, RATE_MID)):
        span_devices = min(SEG_ROWS * spacing // row_count, seq_count)
        sparse_count = row_count // spacing
        chooser, query_rows, pair_rows = level_setup(
            query_all, key_all, value_all, level_offsets[level_no], spacing
        )
        buffer = lower_segment(pair_rows, span_devices)
        allowed = segment_mask(sparse_count, span_devices, seq_index % span_devices)
        level_out, level_lse = attend(query_rows, buffer[:, 0], buffer[:, 1], allowed, scale_factor)
        full_out, full_lse = spread_back(level_out, level_lse, chooser)
        full_outs.append(full_out)
        full_lses.append(full_lse)
    spacing = RATE_TOP
    span_devices = min(SEG_ROWS * spacing // row_count, seq_count)
    sparse_count = row_count // spacing
    chooser, query_rows, pair_rows = level_setup(
        query_all, key_all, value_all, level_offsets[2], spacing
    )
    buffer = lower_segment_top(pair_rows, span_devices)
    allowed = segment_mask(sparse_count, span_devices, seq_index % span_devices)
    level_out, level_lse = attend(query_rows, buffer[:, 0], buffer[:, 1], allowed, scale_factor)
    full_out, full_lse = spread_back(level_out, level_lse, chooser)
    full_outs.append(full_out)
    full_lses.append(full_lse)
    lse_stack = jnp.stack(full_lses)
    level_top = jnp.max(lse_stack, axis=0)
    level_weights = jnp.exp(lse_stack - level_top[None])
    mixed_heads = (
        jnp.sum(level_weights[..., None] * jnp.stack(full_outs), axis=0)
        / jnp.sum(level_weights, axis=0)[..., None]
    )
    heads_out = mixed_heads.astype(jnp.bfloat16).reshape(row_count, head_count * head_width)
    projected = jnp.dot(
        lax.all_gather(heads_out, "head", axis=1, tiled=True),
        out_weight,
        preferred_element_type=jnp.float32,
    )
    return projected.astype(jnp.bfloat16)


def solution(mesh):
    return jax.shard_map(
        local,
        mesh=mesh,
        in_specs=(
            P("seq", "head"),
            P("seq", "head"),
            P("seq", "head"),
            P(None, "head"),
            P(None, "head"),
        ),
        out_specs=P("seq", "head"),
        check_vma=False,
    )
```

profile of v0, /device:TPU:25, one launch (start us, length us, event | category | flops | bytes accessed | tf_op | source)
XLA Modules:
  0.0 146.1 jit_solution(71364334517374462)
XLA Ops:
  6.5 1.2 copy.11
  8.0 1.2 copy.12
  10.4 3.1 %collective-permute-start = (bf16[256,2,6,128]{3,0,2,1:T(8,128)(2,1)}, bf16[256,2,6,128]{3,0,2,1:T(8,128)(2,1)S(1)}, u32[]{:S(2)}, u32[]{:S(2)}) collective-permute-start(bf16[256,2,6,128]{3,0,2,1:T(8,128)(2,1)} %pad_maximum_fusion), channel_id=1, source_target_pairs={{0,4},{4,8},{8,12},{12,16},{16,20},{20,24},{24,28},{1,5},{5,9},{9,... | collective-permute-start | bytes 2359304 | tf_op jit(solution)/shard_map/ppermute | solution.py:17
  14.8 1.9 %collective-permute-start.2 = (bf16[32,2,6,128]{3,0,2,1:T(8,128)(2,1)}, bf16[32,2,6,128]{3,0,2,1:T(8,128)(2,1)S(1)}, u32[]{:S(2)}, u32[]{:S(2)}) collective-permute-start(bf16[32,2,6,128]{3,0,2,1:T(8,128)(2,1)} %pad_maximum_fusion.1), channel_id=1, source_target_pairs={{0,4},{4,8},{8,12},{12,16},{16,20},{20,24},{24,28},{1,5},{5,9},{9,... | collective-permute-start | bytes 294920 | tf_op jit(solution)/shard_map/ppermute | solution.py:17
  16.7 1.2 reshape_reshape.25
  18.5 1.2 fusion.11
  19.9 1.9 %collective-permute-start.5 = (bf16[8,2,6,128]{3,0,2,1:T(8,128)(2,1)S(1)}, bf16[8,2,6,128]{3,0,2,1:T(8,128)(2,1)S(1)}, u32[]{:S(2)}, u32[]{:S(2)}) collective-permute-start(bf16[8,2,6,128]{3,0,2,1:T(8,128)(2,1)S(1)} %pad_maximum_fusion.2), channel_id=1, source_target_pairs={{0,4},{4,8},{8,12},{12,16},{16,20},{20,24},{24,28},{1,5},{5,9},{9,... | collective-permute-start | bytes 73736 | tf_op jit(solution)/shard_map/ppermute | solution.py:17
  23.9 10.5 %collective-permute-done.5 = bf16[8,2,6,128]{3,0,2,1:T(8,128)(2,1)S(1)} collective-permute-done((bf16[8,2,6,128]{3,0,2,1:T(8,128)(2,1)S(1)}, bf16[8,2,6,128]{3,0,2,1:T(8,128)(2,1)S(1)}, u32[]{:S(2)}, u32[]{:S(2)}) %collective-permute-start.5) | collective-permute-done | bytes 24608 | tf_op jit(solution)/shard_map/ppermute | solution.py:17
  34.4 1.3 collective-permute-start.6
  36.9 2.3 %collective-permute-done.6 = bf16[16,2,6,128]{3,0,2,1:T(8,128)(2,1)S(1)} collective-permute-done((bf16[16,2,6,128]{3,0,2,1:T(8,128)(2,1)S(1)}, bf16[16,2,6,128]{3,0,2,1:T(8,128)(2,1)S(1)}, u32[]{:S(2)}, u32[]{:S(2)}) %collective-permute-start.6) | collective-permute-done | bytes 49184 | tf_op jit(solution)/shard_map/ppermute | solution.py:17
  39.3 1.3 collective-permute-start.7
  41.3 1.3 collective-permute-start.3
  42.6 4.0 %collective-permute-done.7 = bf16[32,2,6,128]{3,0,2,1:T(8,128)(2,1)S(1)} collective-permute-done((bf16[32,2,6,128]{3,0,2,1:T(8,128)(2,1)S(1)}, bf16[32,2,6,128]{3,0,2,1:T(8,128)(2,1)S(1)}, u32[]{:S(2)}, u32[]{:S(2)}) %collective-permute-start.7) | collective-permute-done | bytes 98336 | tf_op jit(solution)/shard_map/ppermute | solution.py:17
  49.7 1.3 collective-permute-start.4
  51.9 1.3 maximum_maximum_fusion.1
  53.2 1.5 %collective-permute-start.1 = (bf16[512,2,6,128]{3,0,2,1:T(8,128)(2,1)}, bf16[512,2,6,128]{3,0,2,1:T(8,128)(2,1)}, u32[]{:S(2)}, u32[]{:S(2)}) collective-permute-start(bf16[512,2,6,128]{3,0,2,1:T(8,128)(2,1)} %maximum_maximum_fusion.1), channel_id=1, source_target_pairs={{0,8},{4,12},{8,16},{12,20},{16,24},{20,28},{1,9},{5,13},{9,17},{1... | collective-permute-start | bytes 4718600 | tf_op jit(solution)/shard_map/ppermute | solution.py:17
  54.6 12.3 %collective-permute-done.4 = bf16[128,2,6,128]{3,0,2,1:T(8,128)(2,1)S(1)} collective-permute-done((bf16[128,2,6,128]{3,0,2,1:T(8,128)(2,1)S(1)}, bf16[128,2,6,128]{3,0,2,1:T(8,128)(2,1)S(1)}, u32[]{:S(2)}, u32[]{:S(2)}) %collective-permute-start.4) | collective-permute-done | bytes 393248 | tf_op jit(solution)/shard_map/ppermute | solution.py:17
  69.5 27.8 %collective-permute-done.1 = bf16[512,2,6,128]{3,0,2,1:T(8,128)(2,1)} collective-permute-done((bf16[512,2,6,128]{3,0,2,1:T(8,128)(2,1)}, bf16[512,2,6,128]{3,0,2,1:T(8,128)(2,1)}, u32[]{:S(2)}, u32[]{:S(2)}) %collective-permute-start.1) | collective-permute-done | bytes 1572896 | tf_op jit(solution)/shard_map/ppermute | solution.py:17
  97.2 1.5 %maximum_maximum_fusion = bf16[1024,2,6,128]{3,0,2,1:T(8,128)(2,1)S(1)} fusion(bf16[256,1,6,128]{3,0,2,1:T(8,128)(2,1)S(1)} %copy.14, bf16[256,1,6,128]{3,0,2,1:T(8,128)(2,1)S(1)} %copy.13, bf16[256,2,6,128]{3,0,2,1:T(8,128)(2,1)S(1)} %collective-permute-done, bf16[512,2,6,128]{3,0,2,1:T(8,128)(2,1)} %collective-permute-done.1), kind=kLoop, calls=%fused_computation.5 | loop fusion | flops 12582912 | bytes 6291456 | tf_op jit(solution)/shard_map/concatenate | solution.py:46
  98.8 1.1 fusion.1
  99.9 1.3 fusion
  101.2 2.1 %fusion.5 = f32[1,256,6,128]{1,3,2,0:T(8,128)S(1)} fusion(f32[6,1024,256]{2,1,0:T(8,128)S(1)} %get-tuple-element.20, f32[6,256]{1,0:T(8,128)S(1)} %fusion, f32[6,256]{1,0:T(8,128)S(1)} %get-tuple-element.19, pred[256,1024]{0,1:T(8,128)(4,1)S(1)} %copy-done.4, bf16[1024,2,6,128]{3,0,2,1:T(8,128)(2,1)S(1)} %maximum_maximum_fusion), kind=kOutput, calls=%fused_computation.14 | convolution fusion | flops 410517504 | bytes 8929280 | tf_op jit(solution)/shard_map/hqk,khd->qhd/dot_general | solution.py:38
  104.4 28.0 %all-gather.2.cloned.1.call-done = bf16[256,3072]{0,1:T(8,128)(2,1)} async-done(((bf16[256,768]{0,1:T(8,128)(2,1)}), bf16[256,3072]{0,1:T(8,128)(2,1)}) %all-gather.2.cloned.1.call-update) | async-done | bytes 1572880 | tf_op jit(solution)/shard_map/all_gather | solution.py:137
  132.4 6.8 %convolution_convert_fusion = bf16[256,1280]{1,0:T(8,128)(2,1)} fusion(bf16[256,3072]{0,1:T(8,128)(2,1)} %all-gather.2.cloned.1.call-done, bf16[3072,1280]{1,0:T(8,128)(2,1)} %param.9), kind=kOutput, calls=%fused_computation.7 | convolution fusion | flops 2013593600 | bytes 10092544 | tf_op jit(solution)/shard_map/dot_general | solution.py:136
  (81 shorter events, 14.7 us)
Async XLA Ops:
  6.5 7.1 %copy-start = (bf16[256,768]{1,0:T(8,128)(2,1)S(1)}, bf16[256,768]{1,0:T(8,128)(2,1)}, u32[]{:S(2)}) copy-start(bf16[256,768]{1,0:T(8,128)(2,1)} %param.6) | copy-start | bytes 1179652
  6.5 7.4 %copy-start.1 = (bf16[256,768]{1,0:T(8,128)(2,1)S(1)}, bf16[256,768]{1,0:T(8,128)(2,1)}, u32[]{:S(2)}) copy-start(bf16[256,768]{1,0:T(8,128)(2,1)} %param.7) | copy-start | bytes 1179652
  6.5 7.0 %copy-start.6 = (s32[3,6]{1,0:T(4,128)S(1)}, s32[3,6]{1,0:T(4,128)}, u32[]{:S(2)}) copy-start(s32[3,6]{1,0:T(4,128)} %param.8) | copy-start | bytes 220
  6.5 125.9 %all-gather.2.cloned.1.call-start = ((), (), s32[]{:S(2)}) async-start(), calls=%async_computation | async-start | bytes 1966080 | tf_op jit(solution)/shard_map/all_gather | solution.py:137
  9.4 12.5 %copy-start.2 = (bf16[256,768]{1,0:T(8,128)(2,1)S(1)}, bf16[256,768]{1,0:T(8,128)(2,1)}, u32[]{:S(2)}) copy-start(bf16[256,768]{1,0:T(8,128)(2,1)} %param.5) | copy-start | bytes 1179652
  10.4 41.5 %collective-permute-start = (bf16[256,2,6,128]{3,0,2,1:T(8,128)(2,1)}, bf16[256,2,6,128]{3,0,2,1:T(8,128)(2,1)S(1)}, u32[]{:S(2)}, u32[]{:S(2)}) collective-permute-start(bf16[256,2,6,128]{3,0,2,1:T(8,128)(2,1)} %pad_maximum_fusion), channel_id=1, source_target_pairs={{0,4},{4,8},{8,12},{12,16},{16,20},{20,24},{24,28},{1,5},{5,9},{9,... | collective-permute-start | bytes 2359304 | tf_op jit(solution)/shard_map/ppermute | solution.py:17
  14.8 25.8 %collective-permute-start.2 = (bf16[32,2,6,128]{3,0,2,1:T(8,128)(2,1)}, bf16[32,2,6,128]{3,0,2,1:T(8,128)(2,1)S(1)}, u32[]{:S(2)}, u32[]{:S(2)}) collective-permute-start(bf16[32,2,6,128]{3,0,2,1:T(8,128)(2,1)} %pad_maximum_fusion.1), channel_id=1, source_target_pairs={{0,4},{4,8},{8,12},{12,16},{16,20},{20,24},{24,28},{1,5},{5,9},{9,... | collective-permute-start | bytes 294920 | tf_op jit(solution)/shard_map/ppermute | solution.py:17
  19.9 14.5 %collective-permute-start.5 = (bf16[8,2,6,128]{3,0,2,1:T(8,128)(2,1)S(1)}, bf16[8,2,6,128]{3,0,2,1:T(8,128)(2,1)S(1)}, u32[]{:S(2)}, u32[]{:S(2)}) collective-permute-start(bf16[8,2,6,128]{3,0,2,1:T(8,128)(2,1)S(1)} %pad_maximum_fusion.2), channel_id=1, source_target_pairs={{0,4},{4,8},{8,12},{12,16},{16,20},{20,24},{24,28},{1,5},{5,9},{9,... | collective-permute-start | bytes 73736 | tf_op jit(solution)/shard_map/ppermute | solution.py:17
  34.4 4.8 %collective-permute-start.6 = (bf16[16,2,6,128]{3,0,2,1:T(8,128)(2,1)S(1)}, bf16[16,2,6,128]{3,0,2,1:T(8,128)(2,1)S(1)}, u32[]{:S(2)}, u32[]{:S(2)}) collective-permute-start(bf16[16,2,6,128]{3,0,2,1:T(8,128)(2,1)S(1)} %maximum_maximum_fusion.7), channel_id=1, source_target_pairs={{0,8},{4,12},{8,16},{12,20},{16,24},{20,28},{1,9},{5,13},{9,17},{1... | collective-permute-start | bytes 147464 | tf_op jit(solution)/shard_map/ppermute | solution.py:17
  39.3 7.3 %collective-permute-start.7 = (bf16[32,2,6,128]{3,0,2,1:T(8,128)(2,1)S(1)}, bf16[32,2,6,128]{3,0,2,1:T(8,128)(2,1)S(1)}, u32[]{:S(2)}, u32[]{:S(2)}) collective-permute-start(bf16[32,2,6,128]{3,0,2,1:T(8,128)(2,1)S(1)} %maximum_maximum_fusion.6), channel_id=1, source_target_pairs={{0,16},{4,20},{8,24},{12,28},{1,17},{5,21},{9,25},{13,29},{2,18},{... | collective-permute-start | bytes 294920 | tf_op jit(solution)/shard_map/ppermute | solution.py:17
  41.3 7.4 %collective-permute-start.3 = (bf16[64,2,6,128]{3,0,2,1:T(8,128)(2,1)}, bf16[64,2,6,128]{3,0,2,1:T(8,128)(2,1)}, u32[]{:S(2)}, u32[]{:S(2)}) collective-permute-start(bf16[64,2,6,128]{3,0,2,1:T(8,128)(2,1)} %maximum_maximum_fusion.4), channel_id=1, source_target_pairs={{0,8},{4,12},{8,16},{12,20},{16,24},{20,28},{1,9},{5,13},{9,17},{1... | collective-permute-start | bytes 589832 | tf_op jit(solution)/shard_map/ppermute | solution.py:17
  49.7 17.3 %collective-permute-start.4 = (bf16[128,2,6,128]{3,0,2,1:T(8,128)(2,1)S(1)}, bf16[128,2,6,128]{3,0,2,1:T(8,128)(2,1)S(1)}, u32[]{:S(2)}, u32[]{:S(2)}) collective-permute-start(bf16[128,2,6,128]{3,0,2,1:T(8,128)(2,1)S(1)} %maximum_maximum_fusion.3), channel_id=1, source_target_pairs={{0,16},{4,20},{8,24},{12,28},{1,17},{5,21},{9,25},{13,29},{2,18},{... | collective-permute-start | bytes 1179656 | tf_op jit(solution)/shard_map/ppermute | solution.py:17
  53.2 44.1 %collective-permute-start.1 = (bf16[512,2,6,128]{3,0,2,1:T(8,128)(2,1)}, bf16[512,2,6,128]{3,0,2,1:T(8,128)(2,1)}, u32[]{:S(2)}, u32[]{:S(2)}) collective-permute-start(bf16[512,2,6,128]{3,0,2,1:T(8,128)(2,1)} %maximum_maximum_fusion.1), channel_id=1, source_target_pairs={{0,8},{4,12},{8,16},{12,20},{16,24},{20,28},{1,9},{5,13},{9,17},{1... | collective-permute-start | bytes 4718600 | tf_op jit(solution)/shard_map/ppermute | solution.py:17
  69.4 29.3 %copy-start.4 = (pred[256,1024]{0,1:T(8,128)(4,1)S(1)}, pred[256,1024]{0,1:T(8,128)(4,1)}, u32[]{:S(2)}) copy-start(pred[256,1024]{0,1:T(8,128)(4,1)} %fusion.8) | copy-start | bytes 786436
  69.4 29.3 %copy-start.5 = (bf16[256,768]{0,1:T(8,128)(2,1)S(1)}, bf16[256,768]{0,1:T(8,128)(2,1)}, u32[]{:S(2)}) copy-start(bf16[256,768]{0,1:T(8,128)(2,1)} %copy.15) | copy-start | bytes 1179652
  101.2 2.2 %copy-start.3 = (f32[1,256,6,128]{1,3,2,0:T(8,128)S(1)}, f32[1,256,6,128]{1,3,2,0:T(8,128)}, u32[]{:S(2)}) copy-start(f32[1,256,6,128]{1,3,2,0:T(8,128)} %broadcast_multiply_fusion) | copy-start | bytes 2359300
Sparse Core Ops, SparseCore 0:
  104.5 27.8 all-gather.1
where the time goes:
time: 148 us; the launch traced here: 146 us
  waiting for transfers between devices  85.9 us (58%)
  between operations  13.9 us (9%)
  starting transfers between devices  13.6 us (9%)
  matrix products  13.3 us (9%)
  other arithmetic  12.2 us (8%)
  local copies, waits for them, and re-layouts  7.16 us (5%)
    ppermute x8, waiting for transfers between devices, from_behind(): return lax.ppermute(array, axis, pairs)  57.9 us
    all_gather x1, waiting for transfers between devices, local(): lax.all_gather(heads_out, 'head', axis=1, tiled=True)  28 us
    ppermute x8, starting transfers between devices, from_behind(): return lax.ppermute(array, axis, pairs)  13.6 us
    dot_general x1, matrix products, local(): jnp.dot(lax.all_gather(heads_out, 'head', axis=1, tiled=True), out_weight...  6.79 us
    concatenate x5, other arithmetic, lower_segment(): holding = jnp.concatenate([arrived, holding], axis=0)  5.41 us
    unnamed x17, local copies, waits for them, and re-layouts  3.36 us
  transfers between devices with their start and end apart: 9, of which 7 were waited for; matrix products, arithmetic and copies ran while one was open for 10% of the time, Pallas kernels for 0%

commit v1 on v0

v1 whole, which is shorter than its diff:
```python
import functools

import jax
import jax.numpy as jnp
from jax import lax
from jax.experimental import pallas as pl
from jax.experimental.pallas import tpu as pltpu
from jax.sharding import PartitionSpec as P

RATE_MID = 8
RATE_TOP = 32
SEG_ROWS = 1024


NEG_FILL = -1e30


def push_segment(own, slots, sends, recvs, position, span, me):
    def to_later(by):
        return pltpu.make_async_remote_copy(
            src_ref=own,
            dst_ref=slots.at[position],
            send_sem=sends.at[by],
            recv_sem=recvs.at[by],
            device_id={"seq": me + by},
            device_id_type=pl.DeviceIdType.MESH,
        )

    def from_earlier(by):
        return pltpu.make_async_remote_copy(
            src_ref=own,
            dst_ref=slots.at[position - by],
            send_sem=sends.at[by],
            recv_sem=recvs.at[by],
            device_id={"seq": me - by},
            device_id_type=pl.DeviceIdType.MESH,
        )

    def start():
        @pl.loop(1, span)
        def _(by):
            @pl.when(position + by < span)
            def _():
                to_later(by).start()

    def finish():
        @pl.loop(1, span)
        def _(by):
            @pl.when(position >= by)
            def _():
                from_earlier(by).wait_recv()

            @pl.when(position + by < span)
            def _():
                to_later(by).wait_send()

    def fill():
        slots[position] = own[...]

        @pl.loop(1, span)
        def _(by):
            @pl.when(position + by < span)
            def _():
                slots[position + by] = jnp.zeros_like(own)

    return start, fill, finish


def gather_kernel(
    low_span, top_span, key_ref, value_ref, sparse_ref, keys, values, sparse, sends, recvs, sparse_sends, sparse_recvs
):
    me = lax.axis_index("seq")
    low_at, top_at = lax.rem(me, low_span), lax.rem(me, top_span)
    barrier = pltpu.get_barrier_semaphore()

    @pl.loop(1, top_span)
    def _(by):
        peer = me - top_at + lax.rem(top_at + by, top_span)
        pl.semaphore_signal(
            barrier, inc=1, device_id={"seq": peer}, device_id_type=pl.DeviceIdType.MESH
        )

    pl.semaphore_wait(barrier, top_span - 1)
    plans = (
        push_segment(sparse_ref, sparse, sparse_sends, sparse_recvs, top_at, top_span, me),
        push_segment(key_ref, keys, sends.at[0], recvs.at[0], low_at, low_span, me),
        push_segment(value_ref, values, sends.at[1], recvs.at[1], low_at, low_span, me),
    )
    for step in range(3):
        for plan in plans:
            plan[step]()


def gather_segments(key_rows, value_rows, sparse_rows, low_span, top_span):
    vmem = pl.BlockSpec(memory_space=pltpu.VMEM)
    return pl.pallas_call(
        functools.partial(gather_kernel, low_span, top_span),
        out_shape=(
            jax.ShapeDtypeStruct((low_span, *key_rows.shape), key_rows.dtype),
            jax.ShapeDtypeStruct((low_span, *value_rows.shape), value_rows.dtype),
            jax.ShapeDtypeStruct((top_span, *sparse_rows.shape), sparse_rows.dtype),
        ),
        in_specs=[vmem] * 3,
        out_specs=(vmem,) * 3,
        scratch_shapes=[
            pltpu.SemaphoreType.DMA((2, low_span)),
            pltpu.SemaphoreType.DMA((2, low_span)),
            pltpu.SemaphoreType.DMA((top_span,)),
            pltpu.SemaphoreType.DMA((top_span,)),
        ],
        compiler_params=pltpu.CompilerParams(
            collective_id=0, has_side_effects=True, vmem_limit_bytes=40 * 2**20
        ),
    )(key_rows, value_rows, sparse_rows)


def heads_kernel(peers, own, gathered, sends, recvs, relay_sends, relay_recvs):
    me = lax.axis_index("head")
    core, chips = lax.rem(me, 2), peers // 2
    other = me + 1 - 2 * core
    width = own.shape[1]
    barrier = pltpu.get_barrier_semaphore()

    def across(by):
        return lax.rem(me + 2 * by, peers)

    def behind(by):
        return lax.rem(me + peers - 2 * by, peers)

    for peer in [other] + [across(by) for by in range(1, chips)]:
        pl.semaphore_signal(
            barrier, inc=1, device_id={"head": peer}, device_id_type=pl.DeviceIdType.MESH
        )
    pl.semaphore_wait(barrier, chips)

    def columns(index):
        return gathered.at[:, pl.ds(pl.multiple_of(index * width, width), width)]

    def send(source, index, peer, send_sem, recv_sem):
        return pltpu.make_async_remote_copy(
            src_ref=source,
            dst_ref=columns(index),
            send_sem=send_sem,
            recv_sem=recv_sem,
            device_id={"head": peer},
            device_id_type=pl.DeviceIdType.MESH,
        )

    far = [send(own, me, across(by), sends.at[by], recvs.at[by]) for by in range(1, chips)]
    for copy in far:
        copy.start()
    relays = [send(own, me, other, relay_sends.at[0], relay_recvs.at[0])]
    relays[0].start()
    gathered[:, pl.ds(pl.multiple_of(me * width, width), width)] = own[...]
    for by in range(1, chips):
        source = behind(by)
        send(own, source, across(by), sends.at[by], recvs.at[by]).wait_recv()
        relay = send(columns(source), source, other, relay_sends.at[by], relay_recvs.at[by])
        relay.start()
        relays.append(relay)
    for by, relay in enumerate(relays):
        arriving = lax.rem(other + peers - 2 * by, peers)
        send(own, arriving, other, relay_sends.at[by], relay_recvs.at[by]).wait_recv()
        relay.wait_send()
    for copy in far:
        copy.wait_send()


def gather_heads(heads_out):
    peers = lax.axis_size("head")
    rows, width = heads_out.shape
    vmem = pl.BlockSpec(memory_space=pltpu.VMEM)
    return pl.pallas_call(
        functools.partial(heads_kernel, peers),
        out_shape=jax.ShapeDtypeStruct((rows, peers * width), heads_out.dtype),
        in_specs=[vmem],
        out_specs=vmem,
        scratch_shapes=[pltpu.SemaphoreType.DMA((peers // 2,))] * 4,
        compiler_params=pltpu.CompilerParams(
            collective_id=1, has_side_effects=True, vmem_limit_bytes=24 * 2**20
        ),
    )(heads_out)


def pick_rows(states, chooser, spacing):
    row_count, head_count, head_width = states.shape
    grouped = states.reshape(row_count // spacing, spacing, head_count, head_width)
    return jnp.einsum("nrhd,rh->nhd", grouped, chooser, preferred_element_type=jnp.float32).astype(
        jnp.bfloat16
    )


def attend(query_rows, key_rows, value_rows, allowed, scale_factor):
    scores = (
        jnp.einsum("qhd,khd->hqk", query_rows, key_rows, preferred_element_type=jnp.float32)
        * scale_factor
    )
    scores = jnp.where(allowed[None], scores, NEG_FILL)
    highest = jnp.max(scores, axis=2, keepdims=True)
    weights = jnp.exp(scores - highest)
    totals = jnp.sum(weights, axis=2, keepdims=True)
    shares = (weights / totals).astype(jnp.bfloat16)
    result = jnp.einsum("hqk,khd->qhd", shares, value_rows, preferred_element_type=jnp.float32)
    return (result, (highest + jnp.log(totals))[:, :, 0].T)


def segment_mask(sparse_count, span_devices, position):
    shape_pair = (sparse_count, span_devices * sparse_count)
    query_index = lax.broadcasted_iota(jnp.int32, shape_pair, 0)
    key_index = lax.broadcasted_iota(jnp.int32, shape_pair, 1)
    return key_index <= position * sparse_count + query_index


def spread_back(level_out, level_lse, chooser):
    picked = chooser.astype(jnp.float32)
    sparse_count, head_count, head_width = level_out.shape
    row_count = sparse_count * chooser.shape[0]
    full_out = (level_out[:, None, :, :] * picked[None, :, :, None]).reshape(
        row_count, head_count, head_width
    )
    full_lse = jnp.where(chooser[None], level_lse[:, None, :], NEG_FILL).reshape(
        row_count, head_count
    )
    return (full_out, full_lse)


def level_setup(query_all, key_all, value_all, offset_row, spacing):
    head_count = query_all.shape[1]
    chooser = (
        lax.broadcasted_iota(jnp.int32, (spacing, head_count), 0) == (offset_row % spacing)[None, :]
    )
    chooser_bf = chooser.astype(jnp.bfloat16)
    rows = [pick_rows(states, chooser_bf, spacing) for states in (query_all, key_all, value_all)]
    return (chooser, *rows)


def local(queries, key_states, value_states, level_offsets, out_weight):
    row_count = queries.shape[0]
    head_count = level_offsets.shape[1]
    head_width = queries.shape[1] // head_count
    scale_factor = head_width ** (-0.5)
    seq_count = lax.axis_size("seq")
    seq_index = lax.axis_index("seq")
    query_all = queries.reshape(row_count, head_count, head_width)
    key_all = key_states.reshape(row_count, head_count, head_width)
    value_all = value_states.reshape(row_count, head_count, head_width)
    spacings = (1, RATE_MID, RATE_TOP)
    spans = [min(SEG_ROWS * spacing // row_count, seq_count) for spacing in spacings]
    counts = [row_count // spacing for spacing in spacings]
    setups = [
        level_setup(query_all, key_all, value_all, level_offsets[level_no], spacings[level_no])
        for level_no in (1, 2)
    ]
    sparse_rows = jnp.concatenate(
        [rows for setup in setups for rows in setup[2:]], axis=0
    ).reshape(-1, head_count * head_width)
    keys, values, sparse = gather_segments(
        key_states, value_states, sparse_rows, spans[0], spans[2]
    )
    whole_chooser = jnp.ones((1, head_count), dtype=bool)
    levels = [(whole_chooser, query_all, keys, values)]
    first = 0
    for level_no in (1, 2):
        chooser, query_rows = setups[level_no - 1][:2]
        count, span = counts[level_no], spans[level_no]
        held = sparse
        if span < spans[2]:
            begin = (seq_index % spans[2]) // span * span
            held = lax.dynamic_slice_in_dim(sparse, begin, span, axis=0)
        levels.append(
            (chooser, query_rows, held[:, first : first + count], held[:, first + count : first + 2 * count])
        )
        first += 2 * count
    full_outs = []
    full_lses = []
    for level_no, (chooser, query_rows, key_slots, value_slots) in enumerate(levels):
        allowed = segment_mask(counts[level_no], spans[level_no], seq_index % spans[level_no])
        level_out, level_lse = attend(
            query_rows,
            key_slots.reshape(-1, head_count, head_width),
            value_slots.reshape(-1, head_count, head_width),
            allowed,
            scale_factor,
        )
        full_out, full_lse = spread_back(level_out, level_lse, chooser)
        full_outs.append(full_out)
        full_lses.append(full_lse)
    lse_stack = jnp.stack(full_lses)
    level_top = jnp.max(lse_stack, axis=0)
    level_weights = jnp.exp(lse_stack - level_top[None])
    mixed_heads = (
        jnp.sum(level_weights[..., None] * jnp.stack(full_outs), axis=0)
        / jnp.sum(level_weights, axis=0)[..., None]
    )
    heads_out = mixed_heads.astype(jnp.bfloat16).reshape(row_count, head_count * head_width)
    projected = jnp.dot(
        gather_heads(heads_out),
        out_weight,
        preferred_element_type=jnp.float32,
    )
    return projected.astype(jnp.bfloat16)


def solution(mesh):
    return jax.shard_map(
        local,
        mesh=mesh,
        in_specs=(
            P("seq", "head"),
            P("seq", "head"),
            P("seq", "head"),
            P(None, "head"),
            P(None, "head"),
        ),
        out_specs=P("seq", "head"),
        check_vma=False,
    )
```

time: 148 us -> 118 us (0.80)
  the two profiles are of different devices: /device:TPU:25 before, /device:TPU:0 now
where the time goes in v1:
time: 118 us; the launch traced here: 117 us
  Pallas kernels  68.5 us (58%)
  local copies, waits for them, and re-layouts  22.3 us (19%)
  matrix products  18.1 us (15%)
  other arithmetic  7.48 us (6%)
    pallas_call x1, Pallas kernels, gather_segments(): pl.pallas_call(functools.partial(gather_kernel, low_span, top_span), out_...  55.8 us
    pallas_call x1, Pallas kernels, gather_heads(): pl.pallas_call(functools.partial(heads_kernel, peers), out_shape=jax.Shap...  12.7 us
    unnamed x56, local copies, waits for them, and re-layouts  7.65 us
    dot_general x1, matrix products, local(): jnp.dot(gather_heads(heads_out), out_weight, preferred_element_type=jnp.f...  6.26 us
    dot_general x3, matrix products, attend(): jnp.einsum('hqk,khd->qhd', shares, value_rows, preferred_element_type=jnp...  5.1 us
    reshape x3, local copies, waits for them, and re-layouts, local(): key_slots.reshape(-1, head_count, head_width)  4.34 us
    dot_general x3, matrix products, attend(): jnp.einsum('qhd,khd->hqk', query_rows, key_rows, preferred_element_type=j...  3.48 us
    another operation x3, local copies, waits for them, and re-layouts, pick_rows(): states.reshape(row_count // spacing, spacing, head_count, head_width)  3.35 us

profile of v1, /device:TPU:0, one launch (start us, length us, event | category | flops | bytes accessed | tf_op | source)
XLA Modules:
  0.0 117.0 jit_solution(16675629240118747866)
XLA Ops:
  0.0 0.9 iota_compare_fusion
  2.3 1.4 %reshape_reshape.21 = bf16[8,32,6,128]{3,2,1,0:T(8,128)(2,1)S(1)} reshape(bf16[256,768]{1,0:T(8,128)(2,1)} %value_ref.1) | data formatting | bytes 786432 | tf_op jit(solution)/shard_map/reshape;reshape | solution.py:187
  3.9 1.5 %reshape_reshape.20 = bf16[8,32,6,128]{3,2,1,0:T(8,128)(2,1)S(1)} reshape(bf16[256,768]{1,0:T(8,128)(2,1)} %key_ref.1) | data formatting | bytes 786432 | tf_op jit(solution)/shard_map/reshape;reshape | solution.py:187
  6.2 1.2 %fusion.17 = bf16[6,1,32,128]{3,1,2,0:T(2,128)(2,1)S(1)} fusion(pred[8,6,1,1]{0,1,2,3:T(8,128)(4,1)S(1)} %get-tuple-element.21, bf16[256,768]{1,0:T(8,128)(2,1)} %value_ref.1), kind=kOutput, calls=%fused_computation.28 | convolution fusion | flops 393216 | bytes 442416 | tf_op jit(solution)/shard_map/nrhd,rh->nhd/dot_general | solution.py:188
  7.5 1.2 %fusion.19 = bf16[6,1,32,128]{3,1,2,0:T(2,128)(2,1)S(1)} fusion(pred[8,6,1,1]{0,1,2,3:T(8,128)(4,1)S(1)} %get-tuple-element.21, bf16[256,768]{1,0:T(8,128)(2,1)} %key_ref.1), kind=kOutput, calls=%fused_computation.30 | convolution fusion | flops 393216 | bytes 442416 | tf_op jit(solution)/shard_map/nrhd,rh->nhd/dot_general | solution.py:188
  9.0 1.0 copy-done
  10.0 1.0 copy-done.1
  11.0 55.8 %shard_map.55 = (bf16[4,256,768]{2,1,0:T(8,128)(2,1)S(1)}, bf16[4,256,768]{2,1,0:T(8,128)(2,1)S(1)}, bf16[8,80,768]{2,1,0:T(8,128)(2,1)S(1)}) custom-call(bf16[256,768]{1,0:T(8,128)(2,1)S(1)} %copy-done, bf16[256,768]{1,0:T(8,128)(2,1)S(1)} %copy-done.1, bf16[80,768]{1,0:T(8,128)(2,1)S(1)} %bitcast.115), custom_call_target="tpu_custom_call" | custom-call | tf_op jit(solution)/shard_map/pallas_call | solution.py:96
  66.8 1.0 copy-done.2
  67.8 2.8 %reshape.308 = bf16[1024,6,128]{2,1,0:T(8,128)(2,1)} reshape(bf16[4,256,768]{2,1,0:T(8,128)(2,1)S(1)} %get-tuple-element.8) | data formatting | bytes 3145728 | tf_op jit(solution)/shard_map/reshape | solution.py:280
  70.5 0.9 copy.17
  71.5 2.9 %fusion.1 = (f32[6,256]{1,0:T(8,128)S(1)}, f32[6,1024,256]{2,1,0:T(8,128)S(1)}) fusion(pred[256,1024]{0,1:T(8,128)(4,1)} %iota_compare_fusion, bf16[256,6,128]{0,2,1:T(8,128)(2,1)} %bitcast.119, bf16[1024,6,128]{2,1,0:T(8,128)(2,1)} %reshape.308), kind=kOutput, calls=%fused_computation.4 | convolution fusion | flops 407370240 | bytes 8525824 | tf_op jit(solution)/shard_map/qhd,khd->hqk/dot_general | solution.py:195
  74.4 2.6 %copy-done.4 = f32[6,1024,256]{2,1,0:T(8,128)} copy-done((f32[6,1024,256]{2,1,0:T(8,128)}, f32[6,1024,256]{2,1,0:T(8,128)S(1)}, u32[]{:S(2)}) %copy-start.4) | copy-done | bytes 6291480
  77.1 1.3 %fusion = f32[6,256]{1,0:T(8,128)S(1)} fusion(f32[6,1024,256]{2,1,0:T(8,128)S(1)} %get-tuple-element.30, f32[6,256]{1,0:T(8,128)S(1)} %get-tuple-element.29, pred[256,1024]{0,1:T(8,128)(4,1)S(1)} %copy-done.7), kind=kLoop, calls=%fused_computation.3 | loop fusion | flops 6289920 | bytes 6565888 | tf_op jit(solution)/shard_map/reduce_sum | solution.py:201
  78.5 1.0 fusion.60
  79.5 1.4 %reshape.295 = bf16[256,6,128]{2,1,0:T(8,128)(2,1)S(1)} reshape(bf16[8,32,768]{2,1,0:T(8,128)(2,1)} %get-tuple-element.13) | data formatting | bytes 786432 | tf_op jit(solution)/shard_map/reshape | solution.py:280
  85.3 1.2 %fusion.58 = (f32[256,6]{0,1:T(8,128)}, f32[3,256,6]{1,2,0:T(8,128)}) fusion(f32[256,6]{0,1:T(8,128)S(1)} %fusion.46, f32[1,256,6]{1,2,0:T(8,128)S(1)} %select_n.88, f32[1,256,6]{1,2,0:T(8,128)S(1)} %select_n.85, f32[1,256,6]{1,2,0:T(8,128)S(1)} %fusion.47), kind=kLoop, calls=%fused_computation.102 | loop fusion | flops 16896 | bytes 49152 | tf_op jit(solution)/shard_map/reduce_sum | solution.py:293
  86.5 1.0 copy.22
  87.6 1.3 %reshape.297 = bf16[1024,6,128]{0,2,1:T(8,128)(2,1)S(1)} reshape(bf16[4,256,768]{1,0,2:T(4,128)(2,1)S(1)} %copy.22) | data formatting | bytes 3145728 | tf_op jit(solution)/shard_map/reshape | solution.py:281
  89.0 4.7 %fusion.6 = f32[1,256,6,128]{1,3,2,0:T(8,128)S(1)} fusion(bf16[1024,6,128]{0,2,1:T(8,128)(2,1)S(1)} %reshape.297, f32[6,1024,256]{2,1,0:T(8,128)} %copy-done.4, f32[6,256]{1,0:T(8,128)S(1)} %copy-done.13, f32[6,256]{1,0:T(8,128)S(1)} %get-tuple-element.29, pred[256,1024]{0,1:T(8,128)(4,1)} %iota_compare_fusion), kind=kOutput, calls=%fused_computation.11 | convolution fusion | flops 410517504 | bytes 8925184 | tf_op jit(solution)/shard_map/hqk,khd->qhd/dot_general | solution.py:203
  95.0 1.0 reshape.299
  96.7 1.1 fusion.3
  98.1 12.7 %shard_map.56 = bf16[256,3072]{1,0:T(8,128)(2,1)S(1)} custom-call(bf16[256,768]{1,0:T(8,128)(2,1)S(1)} %copy.28.own), custom_call_target="tpu_custom_call" | custom-call | tf_op jit(solution)/shard_map/pallas_call | solution.py:173
  110.8 6.3 %convolution_convert_fusion = bf16[256,1280]{1,0:T(8,128)(2,1)} fusion(bf16[256,3072]{1,0:T(8,128)(2,1)S(1)} %shard_map.56, bf16[3072,1280]{1,0:T(8,128)(2,1)} %param.9), kind=kOutput, calls=%fused_computation.6 | convolution fusion | flops 2013593600 | bytes 10092544 | tf_op jit(solution)/shard_map/dot_general | solution.py:296
  (98 shorter events, 9.2 us)
Async XLA Ops:
  0.0 70.5 %copy-start.5 = (bf16[256,768]{1,0:T(8,128)(2,1)S(1)}, bf16[256,768]{1,0:T(8,128)(2,1)}, u32[]{:S(2)}) copy-start(bf16[256,768]{1,0:T(8,128)(2,1)} %param.5) | copy-start | bytes 1179652
  9.0 1.0 copy-start
  10.0 1.0 copy-start.1
  70.5 6.5 %copy-start.7 = (pred[256,1024]{0,1:T(8,128)(4,1)S(1)}, pred[256,1024]{0,1:T(8,128)(4,1)}, u32[]{:S(2)}) copy-start(pred[256,1024]{0,1:T(8,128)(4,1)} %iota_compare_fusion) | copy-start | bytes 786436
  71.5 7.1 %copy-start.3 = (bf16[8,80,768]{2,1,0:T(8,128)(2,1)S(1)}, bf16[8,80,768]{2,1,0:T(8,128)(2,1)}, u32[]{:S(2)}) copy-start(bf16[8,80,768]{2,1,0:T(8,128)(2,1)} %copy-done.2) | copy-start | bytes 2949124
  74.4 2.7 %copy-start.4 = (f32[6,1024,256]{2,1,0:T(8,128)}, f32[6,1024,256]{2,1,0:T(8,128)S(1)}, u32[]{:S(2)}) copy-start(f32[6,1024,256]{2,1,0:T(8,128)S(1)} %get-tuple-element.30) | copy-start | bytes 18874372
  74.4 7.8 %copy-start.25 = (pred[8,6]{0,1:T(8,128)(4,1)S(1)}, pred[8,6]{0,1:T(8,128)(4,1)}, u32[]{:S(2)}) copy-start(pred[8,6]{0,1:T(8,128)(4,1)} %get-tuple-element.19) | copy-start | bytes 148
  77.1 7.9 %copy-start.26 = (pred[32,6]{0,1:T(8,128)(4,1)S(1)}, pred[32,6]{0,1:T(8,128)(4,1)}, u32[]{:S(2)}) copy-start(pred[32,6]{0,1:T(8,128)(4,1)} %get-tuple-element.22) | copy-start | bytes 580
  78.4 8.1 %copy-start.12 = (f32[6,256]{1,0:T(8,128)}, f32[6,256]{1,0:T(8,128)S(1)}, u32[]{:S(2)}) copy-start(f32[6,256]{1,0:T(8,128)S(1)} %fusion) | copy-start | bytes 18436
  81.5 5.0 %copy-start.14 = (f32[6,32]{1,0:T(8,128)}, f32[6,32]{1,0:T(8,128)S(1)}, u32[]{:S(2)}) copy-start(f32[6,32]{1,0:T(8,128)S(1)} %get-tuple-element.27) | copy-start | bytes 2308
  81.7 2.2 %copy-start.19 = (f32[6,32]{1,0:T(8,128)}, f32[6,32]{1,0:T(8,128)S(1)}, u32[]{:S(2)}) copy-start(f32[6,32]{1,0:T(8,128)S(1)} %fusion.23) | copy-start | bytes 2308
  84.2 2.3 %copy-start.10 = (f32[6,8,64]{2,1,0:T(8,128)}, f32[6,8,64]{2,1,0:T(8,128)S(1)}, u32[]{:S(2)}) copy-start(f32[6,8,64]{2,1,0:T(8,128)S(1)} %get-tuple-element.26) | copy-start | bytes 36868
  84.2 2.3 %copy-start.16 = (f32[6,8]{1,0:T(8,128)}, f32[6,8]{1,0:T(8,128)S(1)}, u32[]{:S(2)}) copy-start(f32[6,8]{1,0:T(8,128)S(1)} %get-tuple-element.25) | copy-start | bytes 580
  86.5 2.4 %copy-start.13 = (f32[6,256]{1,0:T(8,128)S(1)}, f32[6,256]{1,0:T(8,128)}, u32[]{:S(2)}) copy-start(f32[6,256]{1,0:T(8,128)} %copy-done.12) | copy-start | bytes 18436
  88.9 4.8 %copy-start.6 = (bf16[8,32,768]{2,1,0:T(8,128)(2,1)S(1)}, bf16[8,32,768]{2,1,0:T(8,128)(2,1)}, u32[]{:S(2)}) copy-start(bf16[8,32,768]{2,1,0:T(8,128)(2,1)} %get-tuple-element.14) | copy-start | bytes 1179652
  88.9 5.2 %copy-start.9 = (f32[6,32,256]{2,1,0:T(8,128)S(1)}, f32[6,32,256]{2,1,0:T(8,128)}, u32[]{:S(2)}) copy-start(f32[6,32,256]{2,1,0:T(8,128)} %copy-done.8) | copy-start | bytes 589828
  88.9 5.2 %copy-start.15 = (f32[6,32]{1,0:T(8,128)S(1)}, f32[6,32]{1,0:T(8,128)}, u32[]{:S(2)}) copy-start(f32[6,32]{1,0:T(8,128)} %copy-done.14) | copy-start | bytes 2308
  88.9 5.2 %copy-start.20 = (f32[6,32]{1,0:T(8,128)S(1)}, f32[6,32]{1,0:T(8,128)}, u32[]{:S(2)}) copy-start(f32[6,32]{1,0:T(8,128)} %copy-done.19) | copy-start | bytes 2308
  89.0 5.8 %copy-start.22 = (f32[8,6]{0,1:T(8,128)S(1)}, f32[8,6]{0,1:T(8,128)}, u32[]{:S(2)}) copy-start(f32[8,6]{0,1:T(8,128)} %get-tuple-element.20) | copy-start | bytes 580
  93.6 2.4 %copy-start.11 = (f32[6,8,64]{2,1,0:T(8,128)S(1)}, f32[6,8,64]{2,1,0:T(8,128)}, u32[]{:S(2)}) copy-start(f32[6,8,64]{2,1,0:T(8,128)} %copy-done.10) | copy-start | bytes 36868
  93.6 2.4 %copy-start.17 = (f32[6,8]{1,0:T(8,128)S(1)}, f32[6,8]{1,0:T(8,128)}, u32[]{:S(2)}) copy-start(f32[6,8]{1,0:T(8,128)} %copy-done.16) | copy-start | bytes 580
  93.7 2.4 %copy-start.24 = (f32[6,8]{1,0:T(8,128)S(1)}, f32[6,8]{1,0:T(8,128)}, u32[]{:S(2)}) copy-start(f32[6,8]{1,0:T(8,128)} %copy-done.23) | copy-start | bytes 580
  93.7 2.9 %copy-start.21 = (f32[32,6]{0,1:T(8,128)S(1)}, f32[32,6]{0,1:T(8,128)}, u32[]{:S(2)}) copy-start(f32[32,6]{0,1:T(8,128)} %get-tuple-element.23) | copy-start | bytes 2308
  94.2 3.6 %copy-start.18 = (f32[256,6]{0,1:T(8,128)S(1)}, f32[256,6]{0,1:T(8,128)}, u32[]{:S(2)}) copy-start(f32[256,6]{0,1:T(8,128)} %get-tuple-element.11) | copy-start | bytes 18436
  (3 other events, 2.3 us)

commit v2 on v1

--- a/solution.py
+++ b/solution.py
@@ -63,11 +63,76 @@
             def _():
                 slots[position + by] = jnp.zeros_like(own)
 
-    return start, fill, finish
+    return start, fill, lambda: None, finish
+
+
+def relay_segment(own, slots, sems, position, span, me):
+    odd = lax.rem(position, 2)
+    pair = me + 1 - 2 * odd
+    pair_at = position + 1 - 2 * odd
+
+    def copy(source, slot, peer, row, hop):
+        return pltpu.make_async_remote_copy(
+            src_ref=source,
+            dst_ref=slots.at[slot],
+            send_sem=sems.at[row, hop],
+            recv_sem=sems.at[row + 1, hop],
+            device_id={"seq": peer},
+            device_id_type=pl.DeviceIdType.MESH,
+        )
+
+    def start():
+        @pl.when(position + 2 < span)
+        def _():
+            copy(own, position, me + 2, 0, 0).start()
+
+        @pl.when(odd == 0)
+        def _():
+            copy(own, position, pair, 2, 0).start()
+
+    def fill():
+        slots[position] = own[...]
+
+        @pl.loop(1, span)
+        def _(by):
+            @pl.when(position + by < span)
+            def _():
+                slots[position + by] = jnp.zeros_like(own)
+
+    def forward():
+        @pl.loop(1, span // 2)
+        def _(hop):
+            @pl.when(position >= 2 * hop)
+            def _():
+                slot = position - 2 * hop
+                copy(own, slot, me - 2, 0, hop - 1).wait_recv()
+
+                @pl.when(position + 2 < span)
+                def _():
+                    copy(slots.at[slot], slot, me + 2, 0, hop).start()
+
+                copy(slots.at[slot], slot, pair, 2, hop).start()
+
+    def finish():
+        @pl.loop(0, span // 2)
+        def _(hop):
+            @pl.when((pair_at >= 2 * hop) & (pair_at - 2 * hop < position))
+            def _():
+                copy(own, pair_at - 2 * hop, pair, 2, hop).wait_recv()
+
+            @pl.when((position >= 2 * hop) & (position + 2 < span))
+            def _():
+                copy(own, position - 2 * hop, me + 2, 0, hop).wait_send()
+
+            @pl.when((position >= 2 * hop) & (position - 2 * hop < pair_at))
+            def _():
+                copy(own, position - 2 * hop, pair, 2, hop).wait_send()
+
+    return start, fill, forward, finish
 
 
 def gather_kernel(
-    low_span, top_span, key_ref, value_ref, sparse_ref, keys, values, sparse, sends, recvs, sparse_sends, sparse_recvs
+    low_span, top_span, key_ref, value_ref, sparse_ref, keys, values, sparse, sends, recvs, key_sems, sparse_sems
 ):
     me = lax.axis_index("seq")
     low_at, top_at = lax.rem(me, low_span), lax.rem(me, top_span)
@@ -82,11 +147,11 @@
 
     pl.semaphore_wait(barrier, top_span - 1)
     plans = (
-        push_segment(sparse_ref, sparse, sparse_sends, sparse_recvs, top_at, top_span, me),
-        push_segment(key_ref, keys, sends.at[0], recvs.at[0], low_at, low_span, me),
-        push_segment(value_ref, values, sends.at[1], recvs.at[1], low_at, low_span, me),
-    )
-    for step in range(3):
+        relay_segment(sparse_ref, sparse, sparse_sems, top_at, top_span, me),
+        relay_segment(key_ref, keys, key_sems, low_at, low_span, me),
+        push_segment(value_ref, values, sends, recvs, low_at, low_span, me),
+    )
+    for step in range(4):
         for plan in plans:
             plan[step]()
 
@@ -103,10 +168,10 @@
         in_specs=[vmem] * 3,
         out_specs=(vmem,) * 3,
         scratch_shapes=[
-            pltpu.SemaphoreType.DMA((2, low_span)),
-            pltpu.SemaphoreType.DMA((2, low_span)),
-            pltpu.SemaphoreType.DMA((top_span,)),
-            pltpu.SemaphoreType.DMA((top_span,)),
+            pltpu.SemaphoreType.DMA((low_span,)),
+            pltpu.SemaphoreType.DMA((low_span,)),
+            pltpu.SemaphoreType.DMA((4, low_span // 2)),
+            pltpu.SemaphoreType.DMA((4, top_span // 2)),
         ],
         compiler_params=pltpu.CompilerParams(
             collective_id=0, has_side_effects=True, vmem_limit_bytes=40 * 2**20

time: 118 us -> 112 us (0.949)
  the two profiles are of different devices: /device:TPU:0 before, /device:TPU:25 now
where the time goes in v2:
time: 112 us; the launch traced here: 111 us
  Pallas kernels  62.9 us (56%)
  local copies, waits for them, and re-layouts  22.3 us (20%)
  matrix products  18.1 us (16%)
  other arithmetic  7.48 us (7%)
    pallas_call x1, Pallas kernels, gather_segments(): pl.pallas_call(functools.partial(gather_kernel, low_span, top_span), out_...  48.3 us
    pallas_call x1, Pallas kernels, gather_heads(): pl.pallas_call(functools.partial(heads_kernel, peers), out_shape=jax.Shap...  14.5 us
    unnamed x56, local copies, waits for them, and re-layouts  7.65 us
    dot_general x1, matrix products, local(): jnp.dot(gather_heads(heads_out), out_weight, preferred_element_type=jnp.f...  6.26 us
    dot_general x3, matrix products, attend(): jnp.einsum('hqk,khd->qhd', shares, value_rows, preferred_element_type=jnp...  5.1 us
    reshape x3, local copies, waits for them, and re-layouts, local(): key_slots.reshape(-1, head_count, head_width)  4.34 us
    dot_general x3, matrix products, attend(): jnp.einsum('qhd,khd->hqk', query_rows, key_rows, preferred_element_type=j...  3.48 us
    another operation x3, local copies, waits for them, and re-layouts, pick_rows(): states.reshape(row_count // spacing, spacing, head_count, head_width)  3.35 us

profile of v2, /device:TPU:25, one launch (start us, length us, event | category | flops | bytes accessed | tf_op | source)
XLA Modules:
  0.0 111.4 jit_solution(9497698032226327103)
XLA Ops:
  0.0 0.9 iota_compare_fusion
  2.3 1.4 %reshape_reshape.21 = bf16[8,32,6,128]{3,2,1,0:T(8,128)(2,1)S(1)} reshape(bf16[256,768]{1,0:T(8,128)(2,1)} %value_ref.1) | data formatting | bytes 786432 | tf_op jit(solution)/shard_map/reshape;reshape | solution.py:252
  3.9 1.5 %reshape_reshape.20 = bf16[8,32,6,128]{3,2,1,0:T(8,128)(2,1)S(1)} reshape(bf16[256,768]{1,0:T(8,128)(2,1)} %key_ref.1) | data formatting | bytes 786432 | tf_op jit(solution)/shard_map/reshape;reshape | solution.py:252
  6.2 1.2 %fusion.17 = bf16[6,1,32,128]{3,1,2,0:T(2,128)(2,1)S(1)} fusion(pred[8,6,1,1]{0,1,2,3:T(8,128)(4,1)S(1)} %get-tuple-element.21, bf16[256,768]{1,0:T(8,128)(2,1)} %value_ref.1), kind=kOutput, calls=%fused_computation.28 | convolution fusion | flops 393216 | bytes 442416 | tf_op jit(solution)/shard_map/nrhd,rh->nhd/dot_general | solution.py:253
  7.5 1.2 %fusion.19 = bf16[6,1,32,128]{3,1,2,0:T(2,128)(2,1)S(1)} fusion(pred[8,6,1,1]{0,1,2,3:T(8,128)(4,1)S(1)} %get-tuple-element.21, bf16[256,768]{1,0:T(8,128)(2,1)} %key_ref.1), kind=kOutput, calls=%fused_computation.30 | convolution fusion | flops 393216 | bytes 442416 | tf_op jit(solution)/shard_map/nrhd,rh->nhd/dot_general | solution.py:253
  9.0 1.0 copy-done
  10.0 1.0 copy-done.1
  11.0 48.3 %shard_map.55 = (bf16[4,256,768]{2,1,0:T(8,128)(2,1)S(1)}, bf16[4,256,768]{2,1,0:T(8,128)(2,1)S(1)}, bf16[8,80,768]{2,1,0:T(8,128)(2,1)S(1)}) custom-call(bf16[256,768]{1,0:T(8,128)(2,1)S(1)} %copy-done, bf16[256,768]{1,0:T(8,128)(2,1)S(1)} %copy-done.1, bf16[80,768]{1,0:T(8,128)(2,1)S(1)} %bitcast.115), custom_call_target="tpu_custom_call" | custom-call | tf_op jit(solution)/shard_map/pallas_call | solution.py:161
  59.3 1.0 copy-done.2
  60.3 2.8 %reshape.308 = bf16[1024,6,128]{2,1,0:T(8,128)(2,1)} reshape(bf16[4,256,768]{2,1,0:T(8,128)(2,1)S(1)} %get-tuple-element.8) | data formatting | bytes 3145728 | tf_op jit(solution)/shard_map/reshape | solution.py:345
  63.0 0.9 copy.17
  63.9 2.9 %fusion.1 = (f32[6,256]{1,0:T(8,128)S(1)}, f32[6,1024,256]{2,1,0:T(8,128)S(1)}) fusion(pred[256,1024]{0,1:T(8,128)(4,1)} %iota_compare_fusion, bf16[256,6,128]{0,2,1:T(8,128)(2,1)} %bitcast.119, bf16[1024,6,128]{2,1,0:T(8,128)(2,1)} %reshape.308), kind=kOutput, calls=%fused_computation.4 | convolution fusion | flops 407370240 | bytes 8525824 | tf_op jit(solution)/shard_map/qhd,khd->hqk/dot_general | solution.py:260
  66.9 2.6 %copy-done.4 = f32[6,1024,256]{2,1,0:T(8,128)} copy-done((f32[6,1024,256]{2,1,0:T(8,128)}, f32[6,1024,256]{2,1,0:T(8,128)S(1)}, u32[]{:S(2)}) %copy-start.4) | copy-done | bytes 6291480
  69.6 1.3 %fusion = f32[6,256]{1,0:T(8,128)S(1)} fusion(f32[6,1024,256]{2,1,0:T(8,128)S(1)} %get-tuple-element.30, f32[6,256]{1,0:T(8,128)S(1)} %get-tuple-element.29, pred[256,1024]{0,1:T(8,128)(4,1)S(1)} %copy-done.7), kind=kLoop, calls=%fused_computation.3 | loop fusion | flops 6289920 | bytes 6565888 | tf_op jit(solution)/shard_map/reduce_sum | solution.py:266
  71.0 1.0 fusion.60
  72.0 1.4 %reshape.295 = bf16[256,6,128]{2,1,0:T(8,128)(2,1)S(1)} reshape(bf16[8,32,768]{2,1,0:T(8,128)(2,1)} %get-tuple-element.13) | data formatting | bytes 786432 | tf_op jit(solution)/shard_map/reshape | solution.py:345
  77.8 1.2 %fusion.58 = (f32[256,6]{0,1:T(8,128)}, f32[3,256,6]{1,2,0:T(8,128)}) fusion(f32[256,6]{0,1:T(8,128)S(1)} %fusion.46, f32[1,256,6]{1,2,0:T(8,128)S(1)} %select_n.88, f32[1,256,6]{1,2,0:T(8,128)S(1)} %select_n.85, f32[1,256,6]{1,2,0:T(8,128)S(1)} %fusion.47), kind=kLoop, calls=%fused_computation.102 | loop fusion | flops 16896 | bytes 49152 | tf_op jit(solution)/shard_map/reduce_sum | solution.py:358
  79.0 1.0 copy.22
  80.1 1.3 %reshape.297 = bf16[1024,6,128]{0,2,1:T(8,128)(2,1)S(1)} reshape(bf16[4,256,768]{1,0,2:T(4,128)(2,1)S(1)} %copy.22) | data formatting | bytes 3145728 | tf_op jit(solution)/shard_map/reshape | solution.py:346
  81.4 4.7 %fusion.6 = f32[1,256,6,128]{1,3,2,0:T(8,128)S(1)} fusion(bf16[1024,6,128]{0,2,1:T(8,128)(2,1)S(1)} %reshape.297, f32[6,1024,256]{2,1,0:T(8,128)} %copy-done.4, f32[6,256]{1,0:T(8,128)S(1)} %copy-done.13, f32[6,256]{1,0:T(8,128)S(1)} %get-tuple-element.29, pred[256,1024]{0,1:T(8,128)(4,1)} %iota_compare_fusion), kind=kOutput, calls=%fused_computation.11 | convolution fusion | flops 410517504 | bytes 8925184 | tf_op jit(solution)/shard_map/hqk,khd->qhd/dot_general | solution.py:268
  87.5 1.0 reshape.299
  89.2 1.1 fusion.3
  90.5 14.5 %shard_map.56 = bf16[256,3072]{1,0:T(8,128)(2,1)S(1)} custom-call(bf16[256,768]{1,0:T(8,128)(2,1)S(1)} %copy.28.own), custom_call_target="tpu_custom_call" | custom-call | tf_op jit(solution)/shard_map/pallas_call | solution.py:238
  105.1 6.3 %convolution_convert_fusion = bf16[256,1280]{1,0:T(8,128)(2,1)} fusion(bf16[256,3072]{1,0:T(8,128)(2,1)S(1)} %shard_map.56, bf16[3072,1280]{1,0:T(8,128)(2,1)} %param.9), kind=kOutput, calls=%fused_computation.6 | convolution fusion | flops 2013593600 | bytes 10092544 | tf_op jit(solution)/shard_map/dot_general | solution.py:361
  (98 shorter events, 9.2 us)
Async XLA Ops:
  0.0 63.0 %copy-start.5 = (bf16[256,768]{1,0:T(8,128)(2,1)S(1)}, bf16[256,768]{1,0:T(8,128)(2,1)}, u32[]{:S(2)}) copy-start(bf16[256,768]{1,0:T(8,128)(2,1)} %param.5) | copy-start | bytes 1179652
  9.0 1.0 copy-start
  10.0 1.0 copy-start.1
  63.0 6.5 %copy-start.7 = (pred[256,1024]{0,1:T(8,128)(4,1)S(1)}, pred[256,1024]{0,1:T(8,128)(4,1)}, u32[]{:S(2)}) copy-start(pred[256,1024]{0,1:T(8,128)(4,1)} %iota_compare_fusion) | copy-start | bytes 786436
  63.9 7.1 %copy-start.3 = (bf16[8,80,768]{2,1,0:T(8,128)(2,1)S(1)}, bf16[8,80,768]{2,1,0:T(8,128)(2,1)}, u32[]{:S(2)}) copy-start(bf16[8,80,768]{2,1,0:T(8,128)(2,1)} %copy-done.2) | copy-start | bytes 2949124
  66.9 2.7 %copy-start.4 = (f32[6,1024,256]{2,1,0:T(8,128)}, f32[6,1024,256]{2,1,0:T(8,128)S(1)}, u32[]{:S(2)}) copy-start(f32[6,1024,256]{2,1,0:T(8,128)S(1)} %get-tuple-element.30) | copy-start | bytes 18874372
  66.9 7.8 %copy-start.25 = (pred[8,6]{0,1:T(8,128)(4,1)S(1)}, pred[8,6]{0,1:T(8,128)(4,1)}, u32[]{:S(2)}) copy-start(pred[8,6]{0,1:T(8,128)(4,1)} %get-tuple-element.19) | copy-start | bytes 148
  69.5 7.9 %copy-start.26 = (pred[32,6]{0,1:T(8,128)(4,1)S(1)}, pred[32,6]{0,1:T(8,128)(4,1)}, u32[]{:S(2)}) copy-start(pred[32,6]{0,1:T(8,128)(4,1)} %get-tuple-element.22) | copy-start | bytes 580
  70.9 8.1 %copy-start.12 = (f32[6,256]{1,0:T(8,128)}, f32[6,256]{1,0:T(8,128)S(1)}, u32[]{:S(2)}) copy-start(f32[6,256]{1,0:T(8,128)S(1)} %fusion) | copy-start | bytes 18436
  74.0 5.0 %copy-start.14 = (f32[6,32]{1,0:T(8,128)}, f32[6,32]{1,0:T(8,128)S(1)}, u32[]{:S(2)}) copy-start(f32[6,32]{1,0:T(8,128)S(1)} %get-tuple-element.27) | copy-start | bytes 2308
  74.2 2.2 %copy-start.19 = (f32[6,32]{1,0:T(8,128)}, f32[6,32]{1,0:T(8,128)S(1)}, u32[]{:S(2)}) copy-start(f32[6,32]{1,0:T(8,128)S(1)} %fusion.23) | copy-start | bytes 2308
  76.6 2.3 %copy-start.10 = (f32[6,8,64]{2,1,0:T(8,128)}, f32[6,8,64]{2,1,0:T(8,128)S(1)}, u32[]{:S(2)}) copy-start(f32[6,8,64]{2,1,0:T(8,128)S(1)} %get-tuple-element.26) | copy-start | bytes 36868
  76.6 2.3 %copy-start.16 = (f32[6,8]{1,0:T(8,128)}, f32[6,8]{1,0:T(8,128)S(1)}, u32[]{:S(2)}) copy-start(f32[6,8]{1,0:T(8,128)S(1)} %get-tuple-element.25) | copy-start | bytes 580
  79.0 2.4 %copy-start.13 = (f32[6,256]{1,0:T(8,128)S(1)}, f32[6,256]{1,0:T(8,128)}, u32[]{:S(2)}) copy-start(f32[6,256]{1,0:T(8,128)} %copy-done.12) | copy-start | bytes 18436
  81.4 4.8 %copy-start.6 = (bf16[8,32,768]{2,1,0:T(8,128)(2,1)S(1)}, bf16[8,32,768]{2,1,0:T(8,128)(2,1)}, u32[]{:S(2)}) copy-start(bf16[8,32,768]{2,1,0:T(8,128)(2,1)} %get-tuple-element.14) | copy-start | bytes 1179652
  81.4 5.2 %copy-start.9 = (f32[6,32,256]{2,1,0:T(8,128)S(1)}, f32[6,32,256]{2,1,0:T(8,128)}, u32[]{:S(2)}) copy-start(f32[6,32,256]{2,1,0:T(8,128)} %copy-done.8) | copy-start | bytes 589828
  81.4 5.2 %copy-start.15 = (f32[6,32]{1,0:T(8,128)S(1)}, f32[6,32]{1,0:T(8,128)}, u32[]{:S(2)}) copy-start(f32[6,32]{1,0:T(8,128)} %copy-done.14) | copy-start | bytes 2308
  81.4 5.2 %copy-start.20 = (f32[6,32]{1,0:T(8,128)S(1)}, f32[6,32]{1,0:T(8,128)}, u32[]{:S(2)}) copy-start(f32[6,32]{1,0:T(8,128)} %copy-done.19) | copy-start | bytes 2308
  81.4 5.8 %copy-start.22 = (f32[8,6]{0,1:T(8,128)S(1)}, f32[8,6]{0,1:T(8,128)}, u32[]{:S(2)}) copy-start(f32[8,6]{0,1:T(8,128)} %get-tuple-element.20) | copy-start | bytes 580
  86.1 2.4 %copy-start.11 = (f32[6,8,64]{2,1,0:T(8,128)S(1)}, f32[6,8,64]{2,1,0:T(8,128)}, u32[]{:S(2)}) copy-start(f32[6,8,64]{2,1,0:T(8,128)} %copy-done.10) | copy-start | bytes 36868
  86.1 2.4 %copy-start.17 = (f32[6,8]{1,0:T(8,128)S(1)}, f32[6,8]{1,0:T(8,128)}, u32[]{:S(2)}) copy-start(f32[6,8]{1,0:T(8,128)} %copy-done.16) | copy-start | bytes 580
  86.1 2.4 %copy-start.24 = (f32[6,8]{1,0:T(8,128)S(1)}, f32[6,8]{1,0:T(8,128)}, u32[]{:S(2)}) copy-start(f32[6,8]{1,0:T(8,128)} %copy-done.23) | copy-start | bytes 580
  86.1 2.9 %copy-start.21 = (f32[32,6]{0,1:T(8,128)S(1)}, f32[32,6]{0,1:T(8,128)}, u32[]{:S(2)}) copy-start(f32[32,6]{0,1:T(8,128)} %get-tuple-element.23) | copy-start | bytes 2308
  86.7 3.6 %copy-start.18 = (f32[256,6]{0,1:T(8,128)S(1)}, f32[256,6]{0,1:T(8,128)}, u32[]{:S(2)}) copy-start(f32[256,6]{0,1:T(8,128)} %get-tuple-element.11) | copy-start | bytes 18436
  (3 other events, 2.3 us)

commit v3 on v2

--- a/solution.py
+++ b/solution.py
@@ -267,6 +267,40 @@
     shares = (weights / totals).astype(jnp.bfloat16)
     result = jnp.einsum("hqk,khd->qhd", shares, value_rows, preferred_element_type=jnp.float32)
     return (result, (highest + jnp.log(totals))[:, :, 0].T)
+
+
+def dense_kernel(scale_factor, position_ref, query_ref, key_ref, value_ref, out_ref, lse_ref):
+    rows, held = query_ref.shape[0], key_ref.shape[0]
+    scores = lax.dot_general(
+        query_ref[...], key_ref[...], (((1,), (1,)), ((), ())), preferred_element_type=jnp.float32
+    )
+    query_index = lax.broadcasted_iota(jnp.int32, (rows, held), 0)
+    key_index = lax.broadcasted_iota(jnp.int32, (rows, held), 1)
+    allowed = key_index <= position_ref[0] * rows + query_index
+    scores = jnp.where(allowed, scores * scale_factor, NEG_FILL)
+    highest = jnp.max(scores, axis=1, keepdims=True)
+    weights = jnp.exp(scores - highest)
+    totals = jnp.sum(weights, axis=1, keepdims=True)
+    shares = (weights / totals).astype(jnp.bfloat16)
+    out_ref[...] = jnp.dot(shares, value_ref[...], preferred_element_type=jnp.float32)
+    lse_ref[...] = jnp.broadcast_to(highest + jnp.log(totals), lse_ref.shape)
+
+
+def attend_dense(position, queries, keys, values, head_count, scale_factor):
+    rows, columns = queries.shape
+    width, held = columns // head_count, keys.shape[0]
+    small = pl.BlockSpec((rows, width), lambda head: (0, head))
+    large = pl.BlockSpec((held, width), lambda head: (0, head))
+    out, lse = pl.pallas_call(
+        functools.partial(dense_kernel, scale_factor),
+        grid=(head_count,),
+        out_shape=(jax.ShapeDtypeStruct(queries.shape, jnp.float32),) * 2,
+        in_specs=[pl.BlockSpec(memory_space=pltpu.SMEM), small, large, large],
+        out_specs=(small, small),
+        compiler_params=pltpu.CompilerParams(vmem_limit_bytes=32 * 2**20),
+    )(position.reshape(1), queries, keys, values)
+    by_head = (rows, head_count, width)
+    return out.reshape(by_head), lse.reshape(by_head)[:, :, 0]
 
 
 def segment_mask(sparse_count, span_devices, position):
@@ -322,8 +356,16 @@
     keys, values, sparse = gather_segments(
         key_states, value_states, sparse_rows, spans[0], spans[2]
     )
-    whole_chooser = jnp.ones((1, head_count), dtype=bool)
-    levels = [(whole_chooser, query_all, keys, values)]
+    columns = queries.shape[1]
+    dense_out, dense_lse = attend_dense(
+        seq_index % spans[0],
+        queries,
+        keys.reshape(-1, columns),
+        values.reshape(-1, columns),
+        head_count,
+        scale_factor,
+    )
+    levels = []
     first = 0
     for level_no in (1, 2):
         chooser, query_rows = setups[level_no - 1][:2]
@@ -336,9 +378,9 @@
             (chooser, query_rows, held[:, first : first + count], held[:, first + count : first + 2 * count])
         )
         first += 2 * count
-    full_outs = []
-    full_lses = []
-    for level_no, (chooser, query_rows, key_slots, value_slots) in enumerate(levels):
+    full_outs = [dense_out]
+    full_lses = [dense_lse]
+    for level_no, (chooser, query_rows, key_slots, value_slots) in enumerate(levels, 1):
         allowed = segment_mask(counts[level_no], spans[level_no], seq_index % spans[level_no])
         level_out, level_lse = attend(
             query_rows,

time: 112 us -> 90.3 us (0.81)
  local copies, waits for them, and re-layouts: 22.3 us -> 7.11 us
  matrix products: 18.1 us -> 11.5 us
  Pallas kernels: 62.9 us -> 68.8 us
  other arithmetic: 7.48 us -> 2.16 us
    unnamed x56 -> x9, local copies, waits for them, and re-layouts: 7.65 us -> 0.14 us
    pallas_call x0 -> x1, Pallas kernels: none -> 5.85 us  [attend_dense(): pl.pallas_call(functools.partial(dense_kernel, scale_factor), grid=(head_...]
    dot_general x3 -> x2, matrix products: 5.1 us -> 0.44 us  [attend(): jnp.einsum('hqk,khd->qhd', shares, value_rows, preferred_element_type=jnp...]
    reshape x3 -> x2, local copies, waits for them, and re-layouts: 4.34 us -> 0.59 us  [local(): key_slots.reshape(-1, head_count, head_width)]
    dot_general x3 -> x2, matrix products: 3.48 us -> 0.54 us  [attend(): jnp.einsum('qhd,khd->hqk', query_rows, key_rows, preferred_element_type=j...]
    reshape x3 -> x2, local copies, waits for them, and re-layouts: 2.79 us -> 0.59 us  [local(): value_slots.reshape(-1, head_count, head_width)]
    another operation x3, local copies, waits for them, and re-layouts: 3.35 us -> 1.36 us  [pick_rows(): states.reshape(row_count // spacing, spacing, head_count, head_width)]
    slice x2, local copies, waits for them, and re-layouts: 1.64 us -> 0.1 us  [local(): held[:, first:first + count]]
where the time goes in v3:
time: 90.3 us; the launch traced here: 89.9 us
  Pallas kernels  68.8 us (76%)
  matrix products  11.5 us (13%)
  local copies, waits for them, and re-layouts  7.11 us (8%)
  other arithmetic  2.16 us (2%)
    pallas_call x1, Pallas kernels, gather_segments(): pl.pallas_call(functools.partial(gather_kernel, low_span, top_span), out_...  48.4 us
    pallas_call x1, Pallas kernels, gather_heads(): pl.pallas_call(functools.partial(heads_kernel, peers), out_shape=jax.Shap...  14.5 us
    dot_general x1, matrix products, local(): jnp.dot(gather_heads(heads_out), out_weight, preferred_element_type=jnp.f...  6.26 us
    pallas_call x1, Pallas kernels, attend_dense(): pl.pallas_call(functools.partial(dense_kernel, scale_factor), grid=(head_...  5.85 us
    dot_general x6, matrix products, pick_rows(): jnp.einsum('nrhd,rh->nhd', grouped, chooser, preferred_element_type=jnp.f...  4.28 us

profile of v3, /device:TPU:25, one launch (start us, length us, event | category | flops | bytes accessed | tf_op | source)
XLA Modules:
  0.0 89.9 jit_solution(12687851596909546352)
XLA Ops:
  0.1 0.8 fusion.45
  1.3 1.2 %fusion.11 = bf16[6,1,32,128]{3,1,2,0:T(2,128)(2,1)S(1)} fusion(pred[8,6,1,1]{0,1,2,3:T(8,128)(4,1)S(1)} %get-tuple-element.27, bf16[256,768]{1,0:T(8,128)(2,1)} %value_ref.1), kind=kOutput, calls=%fused_computation.18 | convolution fusion | flops 393216 | bytes 442416 | tf_op jit(solution)/shard_map/nrhd,rh->nhd/dot_general | solution.py:253
  2.6 1.2 %fusion.5 = f32[6,1,32,128]{3,1,2,0:T(1,128)S(1)} fusion(pred[8,6,1,1]{0,1,2,3:T(8,128)(4,1)S(1)} %get-tuple-element.27, bf16[256,768]{1,0:T(8,128)(2,1)} %query_ref.1), kind=kOutput, calls=%fused_computation.12 | convolution fusion | flops 393216 | bytes 491568 | tf_op jit(solution)/shard_map/nrhd,rh->nhd/dot_general | solution.py:253
  3.8 1.2 %fusion.13 = bf16[6,1,32,128]{3,1,2,0:T(2,128)(2,1)S(1)} fusion(pred[8,6,1,1]{0,1,2,3:T(8,128)(4,1)S(1)} %get-tuple-element.27, bf16[256,768]{1,0:T(8,128)(2,1)} %key_ref.1), kind=kOutput, calls=%fused_computation.20 | convolution fusion | flops 393216 | bytes 442416 | tf_op jit(solution)/shard_map/nrhd,rh->nhd/dot_general | solution.py:253
  5.2 0.5 reshape_reshape.23
  5.9 0.5 reshape_reshape.20
  6.5 0.5 reshape_reshape.21
  7.3 48.4 %shard_map.55 = (bf16[4,256,768]{2,1,0:T(8,128)(2,1)S(1)}, bf16[4,256,768]{2,1,0:T(8,128)(2,1)S(1)}, bf16[8,80,768]{2,1,0:T(8,128)(2,1)S(1)}) custom-call(bf16[256,768]{1,0:T(8,128)(2,1)S(1)} %copy-done, bf16[256,768]{1,0:T(8,128)(2,1)S(1)} %copy-done.1, bf16[80,768]{1,0:T(8,128)(2,1)S(1)} %bitcast.101), custom_call_target="tpu_custom_call" | custom-call | tf_op jit(solution)/shard_map/pallas_call | solution.py:161
  55.7 5.9 %shard_map.56 = (f32[256,768]{1,0:T(8,128)S(1)}, f32[256,768]{1,0:T(8,128)S(1)}) custom-call(s32[1]{0:T(128)} %bitcast.position_ref, bf16[256,768]{1,0:T(8,128)(2,1)S(1)} %copy-done.2, bf16[1024,768]{1,0:T(8,128)(2,1)S(1)} %bitcast.99, bf16[1024,768]{1,0:T(8,128)(2,1)S(1)} %bitcast.100), custom_call_target="tpu_custom_call" | custom-call | tf_op jit(solution)/shard_map/pallas_call | solution.py:294
  61.5 1.1 %copy.24 = f32[256,768]{0,1:T(8,128)} copy(f32[256,768]{1,0:T(8,128)S(1)} %get-tuple-element.12) | data formatting | bytes 1572864 | tf_op jit(solution)/shard_map/pallas_call | solution.py:294
  62.7 0.8 slice_bitcast_fusion
  63.7 0.2 fusion.53
  64.5 0.2 convolution_bitcast_fusion.1
  64.7 0.5 reshape.288
  65.2 0.3 fusion.54
  66.1 0.6 copy.28
  66.7 0.5 reshape.290
  67.2 0.2 convolution_bitcast_fusion
  67.5 0.3 copy.31
  67.9 0.3 copy.33
  68.3 0.3 copy.29
  68.6 0.2 fusion
  69.1 14.5 %shard_map.57 = bf16[256,3072]{1,0:T(8,128)(2,1)S(1)} custom-call(bf16[256,768]{1,0:T(8,128)(2,1)S(1)} %copy.34.own), custom_call_target="tpu_custom_call" | custom-call | tf_op jit(solution)/shard_map/pallas_call | solution.py:238
  83.7 6.3 %convolution_convert_fusion = bf16[256,1280]{1,0:T(8,128)(2,1)} fusion(bf16[256,3072]{1,0:T(8,128)(2,1)S(1)} %shard_map.57, bf16[3072,1280]{1,0:T(8,128)(2,1)} %param.9), kind=kOutput, calls=%fused_computation | convolution fusion | flops 2013593600 | bytes 10092544 | tf_op jit(solution)/shard_map/dot_general | solution.py:403
  (47 shorter events, 3.2 us)
Async XLA Ops:
  0.0 5.8 %copy-start = (bf16[256,768]{1,0:T(8,128)(2,1)S(1)}, bf16[256,768]{1,0:T(8,128)(2,1)}, u32[]{:S(2)}) copy-start(bf16[256,768]{1,0:T(8,128)(2,1)} %key_ref.1) | copy-start | bytes 1179652
  0.0 5.2 %copy-start.2 = (bf16[256,768]{1,0:T(8,128)(2,1)S(1)}, bf16[256,768]{1,0:T(8,128)(2,1)}, u32[]{:S(2)}) copy-start(bf16[256,768]{1,0:T(8,128)(2,1)} %query_ref.1) | copy-start | bytes 1179652
  1.2 5.3 %copy-start.1 = (bf16[256,768]{1,0:T(8,128)(2,1)S(1)}, bf16[256,768]{1,0:T(8,128)(2,1)}, u32[]{:S(2)}) copy-start(bf16[256,768]{1,0:T(8,128)(2,1)} %value_ref.1) | copy-start | bytes 1179652
  67.9 0.7 copy-start.3
